TPU v7x, 32 devices: a whole 2x2x4 slice. The times are simulated.
32 devices in a mesh: vocab: 2 (over core), sample: 4 (over y, x), prompt: 4 (over z).
Axes of the slice: x: 2, y: 2, z: 4, core: 2. Of those that a mesh axis runs over, the one named last changes fastest.
Arguments:
- hidden: bfloat16 [1024, 4608], P(('sample', 'prompt'), 'vocab'), may hold values from -12 to 12
- gain: float32 [4608], replicated, may hold values from 0.25 to 1.75
- head: bfloat16 [4608, 64000], P(None, ('vocab', 'sample', 'prompt')), may hold values from -0.25 to 0.25
- candidates: int32 [32, 16], replicated, may hold values from 0 to 63999
- row_prompt: int32 [1024], replicated, may hold values from 0 to 31, as said below
Outputs:
- log_votes: float32 [32, 16], replicated
- row_lse: float32 [1024], P(('sample', 'prompt'))
Inputs may be any that keep to these rules, and one draw needn't show every extreme that they name: `row_prompt`: every prompt has at least one row; the rows of a prompt may stand anywhere among the 1024 rows.
All inputs are finite; a program needn't handle non-finite values.
Results may differ from a plain program's by a relative error of at most 0.00051.
Values may be sent and summed in bfloat16 or wider, within the bound.
A program may use at most 128 MiB of HBM per device.

v0:
```python
import jax
import jax.numpy as jnp
from jax import lax
from jax.sharding import PartitionSpec as P

CAP = 30.0
EPS = 1e-06


def body(hidden, gain, head, candidates, row_prompt):
    width = head.shape[0]
    vocab_dev = head.shape[1]
    shards = lax.axis_size("vocab")
    row_dev = hidden.shape[0]
    cols = hidden.shape[1]
    prompts = candidates.shape[0]
    xf = hidden.astype(jnp.float32)
    squared = lax.psum(jnp.sum(xf * xf, axis=1), "vocab")
    scale = lax.rsqrt(squared / width + EPS)
    gain_part = lax.dynamic_slice_in_dim(gain, lax.axis_index("vocab") * cols, cols)
    normed = (xf * scale[:, None] * gain_part[None, :]).astype(jnp.bfloat16)
    pieces = lax.all_gather(normed[None], ("vocab", "sample", "prompt"), axis=0, tiled=True)
    groups = pieces.shape[0] // shards
    pieces = pieces.reshape(shards, groups, row_dev, cols)
    weight = head.reshape(shards, cols, vocab_dev)
    raw = jnp.einsum("vgrd,vdc->grc", pieces, weight, preferred_element_type=jnp.float32)
    logits = CAP * jnp.tanh(raw.reshape(groups * row_dev, vocab_dev) / CAP)
    rows = logits.shape[0]
    exps = jnp.exp(logits)
    sumexp = jnp.sum(exps, axis=1)
    onehot = (row_prompt[:, None] == jnp.arange(prompts, dtype=jnp.int32)[None, :]).astype(
        jnp.float32
    )
    cands = candidates.shape[1]
    offset = lax.axis_index(("vocab", "sample", "prompt")) * vocab_dev
    cand_local = candidates - offset
    columns = jnp.arange(vocab_dev, dtype=jnp.int32)
    selector = (columns[:, None, None] == cand_local[None, :, :]).astype(jnp.float32)
    selector = selector.reshape(vocab_dev, prompts * cands)
    matched = jnp.dot(
        exps, selector, precision=lax.Precision.HIGHEST, preferred_element_type=jnp.float32
    )
    numer = jnp.einsum(
        "rpc,rp->rc",
        matched.reshape(rows, prompts, cands),
        onehot,
        precision=lax.Precision.HIGHEST,
        preferred_element_type=jnp.float32,
    )
    group = lax.axis_index(("sample", "prompt"))
    totals, numers = lax.psum((sumexp, numer), ("vocab", "sample", "prompt"))
    prob = numers / totals[:, None]
    tally = jnp.dot(
        onehot.T, prob, precision=lax.Precision.HIGHEST, preferred_element_type=jnp.float32
    )
    row_lse = lax.dynamic_slice_in_dim(jnp.log(totals), group * row_dev, row_dev, 0)
    return (jnp.log(tally), row_lse)


def solution(mesh):
    placed = (
        P(("sample", "prompt"), "vocab"),
        P(),
        P(None, ("vocab", "sample", "prompt")),
        P(),
        P(),
    )
    return jax.shard_map(
        body, mesh=mesh, in_specs=placed, out_specs=(P(), P(("sample", "prompt"))), check_vma=False
    )
```

profile of v0, /device:TPU:0, one launch (start us, length us, event | category | flops | bytes accessed | tf_op | source)
XLA Modules:
  0.0 286.3 jit_solution(13338340856101934755)
XLA Ops:
  7.2 0.0 all-gather.3.cloned.1.call-start
  7.2 1.1 fusion.15
  8.3 2.6 psum.21
  10.9 0.8 dynamic_slice.6
  11.7 1.8 fusion.17
  13.5 0.0 all-gather.3.cloned.1.call-update
  13.6 0.0 all-reduce.2.cloned.1.call-start
  13.6 0.7 broadcast_subtract_fusion
  14.3 0.1 copy.10
  14.4 0.9 fusion.18
  15.3 83.0 %all-gather.3.cloned.1.call-done = bf16[2048,2304]{1,0:T(8,128)(2,1)} async-done(((bf16[64,2304]{1,0:T(8,128)(2,1)}), bf16[2048,2304]{1,0:T(8,128)(2,1)}) %all-gather.3.cloned.1.call-update) | async-done | bytes 9437200 | tf_op jit(solution)/shard_map/all_gather | solution.py:22
  98.3 26.6 %fusion.8 = (f32[1024]{0:T(1024)S(1)}, f32[1024,2000,1]{0,1,2:T(8,128)S(1)}) fusion(bf16[1024,2304,2]{1,0,2:T(8,128)(2,1)} %bitcast.35, bf16[250,2,8,2304]{3,2,1,0:T(8,128)(2,1)} %bitcast.34), kind=kOutput, calls=%fused_computation.9 | convolution fusion | flops 18880512000 | bytes 36065280 | tf_op jit(solution)/shard_map/vgrd,vdc->grc/dot_general | solution.py:26
  124.9 8.9 %fusion.3 = f32[1024,32,16]{0,2,1:T(8,128)S(1)} fusion(f32[1024,2000,1]{0,1,2:T(8,128)S(1)} %get-tuple-element.3, s32[32,16]{1,0:T(8,128)S(1)} %copy.10), kind=kOutput, calls=%fused_computation.3 | convolution fusion | flops 12588032000 | bytes 10291200 | tf_op jit(solution)/shard_map/dot_general | solution.py:40
  133.8 0.0 copy-start
  133.8 6.5 %copy.11 = f32[1024,32,16]{1,2,0:T(8,128)} copy(f32[1024,32,16]{0,2,1:T(8,128)S(1)} %fusion.3) | data formatting | bytes 4194304 | tf_op jit(solution)/shard_map/dot_general | solution.py:40
  140.3 10.0 %fusion.13 = f32[1024,1,16]{2,1,0:T(1,128)} fusion(f32[1024,32,16]{1,2,0:T(8,128)} %copy.11, pred[1024,32,1]{1,0,2:T(32,128)(4,1)S(1)} %fusion.18), kind=kOutput, calls=%fused_computation.14 | convolution fusion | flops 6291456 | bytes 2195456 | tf_op jit(solution)/shard_map/rpc,rp->rc/dot_general | solution.py:43
  150.3 0.0 all-reduce.2.cloned.1.call-update
  150.3 39.4 %psum.23 = f32[1024]{0:T(1024)S(1)} all-reduce(f32[1024]{0:T(1024)S(1)} %get-tuple-element.2), channel_id=1, replica_groups=mesh['vocab'=2,'sample'=4,'prompt'=4] {'vocab','sample','prompt'}, use_global_device_ids=true, to_apply=%region_4.0 | all-reduce | flops 1024 | bytes 8192 | tf_op jit(solution)/shard_map/psum | solution.py:51
  189.7 0.6 dynamic_slice.7
  190.3 86.7 %all-reduce.2.cloned.1.call-done = f32[1024,16]{1,0:T(8,128)} async-done(((f32[1024,16]{1,0:T(8,128)}), f32[1024,16]{1,0:T(8,128)}) %all-reduce.2.cloned.1.call-update) | async-done | bytes 65552 | tf_op jit(solution)/shard_map/psum | solution.py:51
  277.0 0.0 copy-done
  277.0 2.5 convolution_log_fusion
  (2 shorter events, 0.0 us)
Async XLA Ops:
  7.2 91.2 %all-gather.3.cloned.1.call-start = ((), (), s32[]{:S(2)}) async-start(), calls=%async_computation.1 | async-start | bytes 9732096 | tf_op jit(solution)/shard_map/all_gather | solution.py:22
  13.6 263.4 %all-reduce.2.cloned.1.call-start = ((), (), s32[]{:S(2)}) async-start(), calls=%async_computation | async-start | bytes 1048576 | tf_op jit(solution)/shard_map/psum | solution.py:51
  133.8 143.2 %copy-start = (s32[1024]{0:T(1024)S(1)}, s32[1024]{0:T(1024)}, u32[]{:S(2)}) copy-start(s32[1024]{0:T(1024)} %param.9) | copy-start | bytes 12292
Sparse Core Ops, SparseCore 0:
  13.7 84.5 all-gather.2
  150.4 126.4 all-reduce.1
where the time goes:
time: 287 us; the launch traced here: 286 us
  waiting for transfers between devices  170 us (59%)
  matrix products  47.9 us (17%)
  blocking collectives  42 us (15%)
  between operations  14.1 us (5%)
  local copies, waits for them, and re-layouts  7.98 us (3%)
  other arithmetic  4.53 us (2%)
    psum x1, waiting for transfers between devices, body(): totals, numers = lax.psum((sumexp, numer), ('vocab', 'sample', 'prompt'))  86.7 us
    all_gather x1, waiting for transfers between devices, body(): lax.all_gather(normed[None], ('vocab', 'sample', 'prompt'), axis=0, tiled...  83 us
    psum x1, blocking collectives, body(): totals, numers = lax.psum((sumexp, numer), ('vocab', 'sample', 'prompt'))  39.4 us
    dot_general x1, matrix products, body(): jnp.einsum('vgrd,vdc->grc', pieces, weight, preferred_element_type=jnp.fl...  26.6 us
    dot_general x1, matrix products, body(): jnp.einsum('rpc,rp->rc', matched.reshape(rows, prompts, cands), onehot, p...  9.97 us
    dot_general x1, matrix products, body(): jnp.dot(exps, selector, precision=lax.Precision.HIGHEST, preferred_elemen...  8.87 us
    dot_general x1, local copies, waits for them, and re-layouts, body(): jnp.dot(exps, selector, precision=lax.Precision.HIGHEST, preferred_elemen...  6.51 us
  transfers between devices with their start and end apart: 2, of which 2 were waited for; matrix products, arithmetic and copies ran while one was open for 1% of the time, Pallas kernels for 0%

commit v1 on v0

v1 whole, which is shorter than its diff:
```python
import functools

import jax
import jax.numpy as jnp
from jax import lax
from jax.experimental import pallas as pl
from jax.experimental.pallas import tpu as pltpu
from jax.sharding import PartitionSpec as P

CAP = 30.0
EPS = 1e-06
AXES = ("vocab", "sample", "prompt")
MESH = pl.DeviceIdType.MESH


def place(flat, sizes):
    return (flat // (sizes[1] * sizes[2]), flat // sizes[2] % sizes[1], flat % sizes[2])


def finish_kernel(
    sizes, sums_ref, terms_ref, tally_ref, totals_ref,
    sums_in, part, part_in, send_a, recv_a, send_b, recv_b,
):
    devices = sizes[0] * sizes[1] * sizes[2]
    me = lax.axis_index(AXES)
    barrier = pltpu.get_barrier_semaphore()

    def greet(step, carry):
        peer = (me + step) % devices
        pl.semaphore_signal(barrier, inc=1, device_id=place(peer, sizes), device_id_type=MESH)
        return carry

    lax.fori_loop(1, devices, greet, 0)
    pl.semaphore_wait(barrier, devices - 1)

    def push(source, target, send_sem, recv_sem):
        def out(step, carry):
            peer = (me + step) % devices
            pltpu.make_async_remote_copy(
                src_ref=source,
                dst_ref=target.at[me],
                send_sem=send_sem.at[step],
                recv_sem=recv_sem.at[me],
                device_id=place(peer, sizes),
                device_id_type=MESH,
            ).start()
            return carry

        lax.fori_loop(1, devices, out, 0)

    def collect(source, target, send_sem, recv_sem):
        def arrive(step, carry):
            peer = (me + step) % devices
            pltpu.make_async_remote_copy(
                src_ref=source,
                dst_ref=target.at[peer],
                send_sem=send_sem.at[step],
                recv_sem=recv_sem.at[peer],
                device_id=place(peer, sizes),
                device_id_type=MESH,
            ).wait()
            return carry

        lax.fori_loop(1, devices, arrive, 0)

    push(sums_ref, sums_in, send_a, recv_a)
    sums_in[me] = sums_ref[...]
    collect(sums_ref, sums_in, send_a, recv_a)
    total = jnp.sum(sums_in[...], axis=0)
    totals_ref[...] = total
    part[...] = jnp.dot(
        1.0 / total, terms_ref[...],
        precision=lax.Precision.HIGHEST, preferred_element_type=jnp.float32,
    )
    push(part, part_in, send_b, recv_b)
    part_in[me] = part[...]
    collect(part, part_in, send_b, recv_b)
    tally_ref[...] = jnp.log(jnp.sum(part_in[...], axis=0))


def finish(sums, terms):
    sizes = tuple(lax.axis_size(axis) for axis in AXES)
    devices = sizes[0] * sizes[1] * sizes[2]
    rows, picks = terms.shape
    vmem = pl.BlockSpec(memory_space=pltpu.VMEM)
    return pl.pallas_call(
        functools.partial(finish_kernel, sizes),
        out_shape=(
            jax.ShapeDtypeStruct((1, picks), jnp.float32),
            jax.ShapeDtypeStruct((1, rows), jnp.float32),
        ),
        in_specs=[vmem] * 2,
        out_specs=(vmem, vmem),
        scratch_shapes=[
            pltpu.VMEM((devices, 1, rows), jnp.float32),
            pltpu.VMEM((1, picks), jnp.float32),
            pltpu.VMEM((devices, 1, picks), jnp.float32),
            pltpu.SemaphoreType.DMA((devices,)),
            pltpu.SemaphoreType.DMA((devices,)),
            pltpu.SemaphoreType.DMA((devices,)),
            pltpu.SemaphoreType.DMA((devices,)),
        ],
        compiler_params=pltpu.CompilerParams(
            collective_id=1, has_side_effects=True, vmem_limit_bytes=24 << 20
        ),
    )(sums, terms)


def plain_head(hidden, gain, head, wanted, row_prompt, cands):
    width = head.shape[0]
    vocab_dev = head.shape[1]
    shards = lax.axis_size("vocab")
    row_dev = hidden.shape[0]
    cols = hidden.shape[1]
    xf = hidden.astype(jnp.float32)
    squared = lax.psum(jnp.sum(xf * xf, axis=1), "vocab")
    scale = lax.rsqrt(squared / width + EPS)
    gain_part = lax.dynamic_slice_in_dim(gain, lax.axis_index("vocab") * cols, cols)
    normed = (xf * scale[:, None] * gain_part[None, :]).astype(jnp.bfloat16)
    pieces = lax.all_gather(normed[None], AXES, axis=0, tiled=True)
    groups = pieces.shape[0] // shards
    pieces = pieces.reshape(shards, groups, row_dev, cols)
    weight = head.reshape(shards, cols, vocab_dev)
    raw = jnp.einsum("vgrd,vdc->grc", pieces, weight, preferred_element_type=jnp.float32)
    exps = jnp.exp(CAP * jnp.tanh(raw.reshape(groups * row_dev, vocab_dev) / CAP))
    sums = jnp.sum(exps, axis=1)
    columns = jnp.arange(vocab_dev, dtype=jnp.int32)
    selector = (columns[:, None] == wanted[None, :]).astype(jnp.bfloat16)
    high = lax.reduce_precision(exps, 8, 7)
    low = (exps - high).astype(jnp.bfloat16)
    high = high.astype(jnp.bfloat16)
    picked = jnp.dot(high, selector, preferred_element_type=jnp.float32)
    picked = picked + jnp.dot(low, selector, preferred_element_type=jnp.float32)
    prompt_of = jnp.arange(wanted.shape[0], dtype=jnp.int32) // cands
    terms = jnp.where(row_prompt[:, None] == prompt_of[None, :], picked, 0.0)
    return sums[None, :], terms


def body(hidden, gain, head, candidates, row_prompt):
    row_dev = hidden.shape[0]
    prompts, cands = candidates.shape
    offset = lax.axis_index(AXES) * head.shape[1]
    wanted = candidates.reshape(prompts * cands) - offset
    sums, terms = plain_head(hidden, gain, head, wanted, row_prompt, cands)
    votes, totals = finish(sums, terms)
    group = lax.axis_index(("sample", "prompt"))
    row_lse = lax.dynamic_slice_in_dim(jnp.log(totals[0]), group * row_dev, row_dev, 0)
    return votes.reshape(prompts, cands), row_lse


def solution(mesh):
    placed = (
        P(("sample", "prompt"), "vocab"),
        P(),
        P(None, AXES),
        P(),
        P(),
    )
    return jax.shard_map(
        body, mesh=mesh, in_specs=placed, out_specs=(P(), P(("sample", "prompt"))), check_vma=False
    )
```

time: 287 us -> 157 us (0.55)
  waiting for transfers between devices: 170 us -> 83.9 us
  blocking collectives: 42 us -> 2.59 us
  Pallas kernels: 0 us -> 17 us
  matrix products: 47.9 us -> 32.2 us
  local copies, waits for them, and re-layouts: 7.98 us -> 2.82 us
    psum x1 -> x0, waiting for transfers between devices: 86.7 us -> none  [body(): totals, numers = lax.psum((sumexp, numer), ('vocab', 'sample', 'prompt'))]
    psum x2 -> x1, blocking collectives: 42 us -> 2.59 us  [plain_head(): squared = lax.psum(jnp.sum(xf * xf, axis=1), 'vocab')]
    pallas_call x0 -> x1, Pallas kernels: none -> 17 us  [finish(): pl.pallas_call(functools.partial(finish_kernel, sizes), out_shape=(jax.Sh...]
    dot_general x4 -> x3, matrix products: 47.9 us -> 32.2 us  [the longest x1 26.4 us: plain_head(): jnp.einsum('vgrd,vdc->grc', pieces, weight, preferred_element_type=jnp.fl...]
    dot_general x1 -> x0, local copies, waits for them, and re-layouts: 6.51 us -> none  [body(): jnp.dot(exps, selector, precision=lax.Precision.HIGHEST, preferred_elemen...]
  transfers between devices with their start and end apart: 2 -> 1, of which waited for: 2 -> 1; matrix products, arithmetic and copies ran while one was open for 1% -> 1% of each run, Pallas kernels for 0% -> 0%
where the time goes in v1:
time: 157 us
  waiting for transfers between devices  83.9 us (53%)
  matrix products  32.2 us (21%)
  Pallas kernels  17 us (11%)
  between operations  14.1 us (9%)
  other arithmetic  4.31 us (3%)
  local copies, waits for them, and re-layouts  2.82 us (2%)
  blocking collectives  2.59 us (2%)
    all_gather x1, waiting for transfers between devices, plain_head(): pieces = lax.all_gather(normed[None], AXES, axis=0, tiled=True)  83.9 us
    dot_general x1, matrix products, plain_head(): jnp.einsum('vgrd,vdc->grc', pieces, weight, preferred_element_type=jnp.fl...  26.4 us
    pallas_call x1, Pallas kernels, finish(): pl.pallas_call(functools.partial(finish_kernel, sizes), out_shape=(jax.Sh...  17 us
    dot_general x1, matrix products, plain_head(): picked = picked + jnp.dot(low, selector, preferred_element_type=jnp.float32)  3.29 us
  transfers between devices with their start and end apart: 1, of which 1 were waited for; matrix products, arithmetic and copies ran while one was open for 1% of the time, Pallas kernels for 0%

profile of v1, /device:TPU:0, one launch (start us, length us, event | category | flops | bytes accessed | tf_op | source)
XLA Modules:
  0.0 157.0 jit_solution(2667748592950417355)
XLA Ops:
  7.2 0.0 all-gather.3.cloned.1.call-start
  7.2 1.1 fusion.15
  8.3 2.6 %psum.7 = f32[64]{0:T(128)S(1)} all-reduce(f32[64]{0:T(128)S(1)} %fusion.15), channel_id=1, replica_groups=mesh['vocab'=2,'sample'=4,'prompt'=4] {'vocab'}, use_global_device_ids=true, to_apply=%region_1.0 | all-reduce | flops 64 | bytes 512 | tf_op jit(solution)/shard_map/psum | solution.py:116
  10.9 0.8 dynamic_slice.8
  11.7 1.8 %fusion.17 = bf16[64,2304]{1,0:T(8,128)(2,1)} fusion(bf16[64,2304]{1,0:T(8,128)(2,1)} %param.5, f32[2304]{0:T(1024)S(1)} %dynamic_slice.8, f32[64]{0:T(128)S(1)} %add_rsqrt_fusion), kind=kLoop, calls=%fused_computation.23 | loop fusion | flops 589824 | bytes 599296 | tf_op jit(solution)/shard_map/convert_element_type | solution.py:119
  13.5 0.0 all-gather.3.cloned.1.call-update
  13.6 0.7 broadcast_subtract_fusion
  14.3 0.1 copy.10
  14.4 0.1 sub.25
  14.4 83.9 %all-gather.3.cloned.1.call-done = bf16[2048,2304]{1,0:T(8,128)(2,1)} async-done(((bf16[64,2304]{1,0:T(8,128)(2,1)}), bf16[2048,2304]{1,0:T(8,128)(2,1)}) %all-gather.3.cloned.1.call-update) | async-done | bytes 9437200 | tf_op jit(solution)/shard_map/all_gather | solution.py:120
  98.3 26.4 %fusion.7 = (f32[1024]{0:T(1024)S(1)}, f32[1024,2000,1]{0,1,2:T(8,128)S(1)}) fusion(bf16[1024,2304,2]{1,0,2:T(8,128)(2,1)} %bitcast.35, bf16[250,2,8,2304]{3,2,1,0:T(8,128)(2,1)} %bitcast.34), kind=kOutput, calls=%fused_computation.10 | convolution fusion | flops 18880512000 | bytes 36065280 | tf_op jit(solution)/shard_map/vgrd,vdc->grc/dot_general | solution.py:124
  124.7 0.0 copy-start
  124.7 3.3 %fusion.8 = f32[1024,512]{1,0:T(8,128)S(1)} fusion(f32[1024,2000,1]{0,1,2:T(8,128)S(1)} %get-tuple-element.11, s32[512]{0:T(512)S(1)} %sub.25), kind=kOutput, calls=%fused_computation.12 | convolution fusion | flops 2108416000 | bytes 10291200 | tf_op jit(solution)/shard_map/dot_general | solution.py:133
  128.0 0.0 copy-done
  128.0 2.6 %add_select_fusion.terms_ref = f32[1024,512]{1,0:T(8,128)S(1)} fusion(f32[1024,512]{1,0:T(8,128)S(1)} %fusion.8, s32[512]{0:T(512)S(1)} %sub.25, f32[1024,2000,1]{0,1,2:T(8,128)S(1)} %get-tuple-element.11, s32[512]{0:T(512)S(1)} %add_select_fusion.1, s32[1024]{0:T(1024)S(1)} %copy-done), kind=kOutput, calls=%fused_computation.16 | convolution fusion | flops 2107940864 | bytes 12394496 | tf_op jit(solution)/shard_map/dot_general | solution.py:132
  130.6 17.0 %shard_map.68 = (f32[1,512]{1,0:T(1,128)S(1)}, f32[1,1024]{1,0:T(1,128)S(1)}) custom-call(f32[1,1024]{1,0:T(1,128)S(1)} %bitcast.33, f32[1024,512]{1,0:T(8,128)S(1)} %add_select_fusion.terms_ref), custom_call_target="tpu_custom_call" | custom-call | tf_op jit(solution)/shard_map/pallas_call | solution.py:86
  147.6 0.5 broadcast.68
  148.2 0.7 reduce.3
  148.8 0.1 reshape.43
  148.9 0.7 copy.11
  149.6 0.6 fusion.21
  (2 shorter events, 0.0 us)
Async XLA Ops:
  7.2 91.2 %all-gather.3.cloned.1.call-start = ((), (), s32[]{:S(2)}) async-start(), calls=%async_computation | async-start | bytes 9732096 | tf_op jit(solution)/shard_map/all_gather | solution.py:120
  124.7 3.3 %copy-start = (s32[1024]{0:T(1024)S(1)}, s32[1024]{0:T(1024)}, u32[]{:S(2)}) copy-start(s32[1024]{0:T(1024)} %param.9) | copy-start | bytes 12292
Sparse Core Ops, SparseCore 0:
  13.7 84.5 all-gather.2

commit v2 on v1

--- a/solution.py
+++ b/solution.py
@@ -136,12 +136,236 @@
     return sums[None, :], terms
 
 
+def head_kernel(
+    sizes, cands, hidden_ref, gain_ref, head_hbm, wanted_ref, prompt_ref, sums_ref, terms_ref,
+    gathered, head, selector, mine, theirs,
+    head_sem, square_send, square_recv, line_send, pair_send, first_send, second_send, recv,
+):
+    depth = sizes[2]
+    row_dev, cols = hidden_ref.shape
+    width, vocab_dev = head.shape
+    span = depth * row_dev
+    lanes = mine.shape[1]
+    core = lax.axis_index("vocab")
+    sample = lax.axis_index("sample")
+    spot = lax.axis_index("prompt")
+    near_x = sample + 1 - 2 * (sample % 2)
+    near_y = sample + 2 - 4 * (sample // 2)
+    first = near_x * (1 - core) + near_y * core
+    second = near_y * (1 - core) + near_x * core
+    across = 3 - sample
+
+    pair_at = (1 - core, sample, spot)
+    first_at = (core, first, spot)
+    second_at = (core, second, spot)
+
+    load = pltpu.make_async_copy(head_hbm, head, head_sem)
+    load.start()
+
+    barrier = pltpu.get_barrier_semaphore()
+    for step in range(1, depth):
+        pl.semaphore_signal(
+            barrier, inc=1, device_id=(core, sample, (spot + step) % depth), device_id_type=MESH
+        )
+    for target in (pair_at, first_at, second_at):
+        pl.semaphore_signal(barrier, inc=1, device_id=target, device_id_type=MESH)
+    pl.semaphore_wait(barrier, depth + 2)
+
+    def block(half, column, at):
+        start = pl.multiple_of((column * depth + at) * row_dev, row_dev)
+        return gathered.at[half, pl.ds(start, row_dev)]
+
+    def copy(half, column, at, send_sem, target):
+        return pltpu.make_async_remote_copy(
+            src_ref=block(half, column, at),
+            dst_ref=block(half, column, at),
+            send_sem=send_sem,
+            recv_sem=recv.at[half, column * depth + at],
+            device_id=target,
+            device_id_type=MESH,
+        )
+
+    def arrived(half, column, at):
+        copy(half, column, at, pair_send.at[0], pair_at).wait_recv()
+
+    def to_pair(column, at):
+        copy(core, column, at, pair_send.at[column * depth + at], pair_at).start()
+
+    def to_first(at):
+        copy(core, sample, at, first_send.at[at], first_at).start()
+
+    def to_second(column, at, turn):
+        copy(core, column, at, second_send.at[turn, at], second_at).start()
+
+    xf = hidden_ref[...].astype(jnp.float32)
+    squares = xf[:, :lanes] * xf[:, :lanes]
+    for begin in range(lanes, cols, lanes):
+        squares = squares + xf[:, begin : begin + lanes] * xf[:, begin : begin + lanes]
+    mine[...] = squares
+    swap = pltpu.make_async_remote_copy(
+        src_ref=mine, dst_ref=theirs, send_sem=square_send, recv_sem=square_recv,
+        device_id=pair_at, device_id_type=MESH,
+    )
+    swap.start()
+    swap.wait()
+    squared = jnp.sum(mine[...] + theirs[...], axis=1, keepdims=True)
+    scale = lax.rsqrt(squared / width + EPS)
+    own = pl.multiple_of((sample * depth + spot) * row_dev, row_dev)
+    gathered[core, pl.ds(own, row_dev), :] = (
+        hidden_ref[...].astype(jnp.float32) * scale * gain_ref[core]
+    ).astype(jnp.bfloat16)
+
+    to_first(spot)
+    to_second(sample, spot, 0)
+    for step in range(1, depth):
+        at = (spot + step) % depth
+        copy(core, sample, spot, line_send.at[step], (core, sample, at)).start()
+    to_pair(sample, spot)
+
+    picks = wanted_ref.shape[1]
+    rows_of = lax.broadcasted_iota(jnp.int32, (vocab_dev, picks), 0)
+    selector[...] = jnp.where(rows_of == wanted_ref[...], 1.0, 0.0).astype(jnp.bfloat16)
+
+    for step in (1, depth - 1, *range(2, depth - 1)):
+        at = (spot + step) % depth
+        arrived(core, sample, at)
+        to_first(at)
+        to_second(sample, at, 0)
+        to_pair(sample, at)
+
+    def pass_on(column, at):
+        arrived(core, column, at)
+        to_pair(column, at)
+
+    steps = [(begin, min(begin + 512, vocab_dev)) for begin in range(0, vocab_dev, 512)]
+    count = len(steps)
+    order = [0, 1, depth - 1, *range(2, depth - 1)]
+
+    def turn(t, carry):
+        column = jnp.where(
+            t == 0, sample, jnp.where(t == 1, near_x, jnp.where(t == 2, near_y, across))
+        )
+        start = pl.multiple_of(column * span, span)
+
+        @pl.when(t == 0)
+        def _():
+            load.wait()
+            for step in range(depth):
+                arrived(1 - core, sample, (spot + step) % depth)
+
+        @pl.when(t == 1)
+        def _():
+            for step in order:
+                pass_on(second, (spot + step) % depth)
+            for step in range(depth):
+                arrived(1 - core, first, (spot + step) % depth)
+                arrived(1 - core, second, (spot + step) % depth)
+
+        @pl.when(t == 3)
+        def _():
+            for step in range(depth):
+                arrived(1 - core, across, (spot + step) % depth)
+
+        total = jnp.zeros((span, 1), jnp.float32)
+        found = None
+        for index, (begin, end) in enumerate(steps):
+            portion = range(depth * index // count, depth * (index + 1) // count)
+
+            @pl.when(t == 0)
+            def _():
+                for step in portion:
+                    at = (spot + order[step]) % depth
+                    arrived(core, first, at)
+                    to_second(first, at, 1)
+                    to_pair(first, at)
+
+            raw = jnp.dot(
+                gathered[0, pl.ds(start, span), :], head[:cols, begin:end],
+                preferred_element_type=jnp.float32,
+            ) + jnp.dot(
+                gathered[1, pl.ds(start, span), :], head[cols:, begin:end],
+                preferred_element_type=jnp.float32,
+            )
+            exps = jnp.exp(CAP * jnp.tanh(raw / CAP))
+            total = total + jnp.sum(exps, axis=1, keepdims=True)
+            high = exps.astype(jnp.bfloat16)
+            low = (exps - high.astype(jnp.float32)).astype(jnp.bfloat16)
+            part = jnp.dot(
+                high, selector[begin:end, :], preferred_element_type=jnp.float32
+            ) + jnp.dot(low, selector[begin:end, :], preferred_element_type=jnp.float32)
+            found = part if found is None else found + part
+
+            for step in range(depth):
+                if (2 * count * (step + 1) - 1) // depth % count == index:
+
+                    @pl.when(t == 1 + (2 * count * (step + 1) - 1) // depth // count)
+                    def _():
+                        pass_on(across, (spot + order[step]) % depth)
+
+        prompt_of = lax.broadcasted_iota(jnp.int32, (span, picks), 1) // cands
+        terms_ref[pl.ds(start, span), :] = jnp.where(
+            prompt_ref[pl.ds(start, span), :] == prompt_of, found, 0.0
+        )
+        sums_ref[column] = jnp.transpose(jnp.broadcast_to(total, (span, lanes)))[:1, :]
+        return carry
+
+    lax.fori_loop(0, 4, turn, 0)
+
+    for step in range(1, depth):
+        copy(core, sample, spot, line_send.at[step], pair_at).wait_send()
+    for at in range(depth):
+        copy(core, sample, at, first_send.at[at], first_at).wait_send()
+        copy(core, sample, at, second_send.at[0, at], second_at).wait_send()
+        copy(core, first, at, second_send.at[1, at], second_at).wait_send()
+        for column in range(sizes[1]):
+            copy(core, column, at, pair_send.at[column * depth + at], pair_at).wait_send()
+
+
+def fused_head(hidden, gain, head, wanted, row_prompt, cands):
+    sizes = tuple(lax.axis_size(axis) for axis in AXES)
+    row_dev, cols = hidden.shape
+    rows, picks = row_prompt.shape[0], wanted.shape[0]
+    groups = sizes[1] * sizes[2]
+    span = sizes[2] * row_dev
+    lanes = 128
+    vmem = pl.BlockSpec(memory_space=pltpu.VMEM)
+    dma = pltpu.SemaphoreType.DMA
+    sums, terms = pl.pallas_call(
+        functools.partial(head_kernel, sizes, cands),
+        out_shape=(
+            jax.ShapeDtypeStruct((sizes[1], 1, span), jnp.float32),
+            jax.ShapeDtypeStruct((rows, picks), jnp.float32),
+        ),
+        in_specs=[vmem, vmem, pl.BlockSpec(memory_space=pl.ANY), vmem, vmem],
+        out_specs=(vmem, vmem),
+        scratch_shapes=[
+            pltpu.VMEM((sizes[0], rows, cols), jnp.bfloat16),
+            pltpu.VMEM(head.shape, jnp.bfloat16),
+            pltpu.VMEM((head.shape[1], picks), jnp.bfloat16),
+            pltpu.VMEM((row_dev, lanes), jnp.float32),
+            pltpu.VMEM((row_dev, lanes), jnp.float32),
+            dma, dma, dma,
+            dma((sizes[2],)),
+            dma((groups,)),
+            dma((sizes[2],)),
+            dma((2, sizes[2])),
+            dma((sizes[0], groups)),
+        ],
+        compiler_params=pltpu.CompilerParams(
+            collective_id=0, has_side_effects=True, vmem_limit_bytes=54 << 20
+        ),
+    )(hidden, gain.reshape(sizes[0], 1, cols), head, wanted[None, :], row_prompt[:, None])
+    return sums.reshape(1, rows), terms
+
+
 def body(hidden, gain, head, candidates, row_prompt):
     row_dev = hidden.shape[0]
     prompts, cands = candidates.shape
     offset = lax.axis_index(AXES) * head.shape[1]
     wanted = candidates.reshape(prompts * cands) - offset
-    sums, terms = plain_head(hidden, gain, head, wanted, row_prompt, cands)
+    corners = lax.axis_size("vocab") == 2 and lax.axis_size("sample") == 4
+    local = fused_head if corners else plain_head
+    sums, terms = local(hidden, gain, head, wanted, row_prompt, cands)
     votes, totals = finish(sums, terms)
     group = lax.axis_index(("sample", "prompt"))
     row_lse = lax.dynamic_slice_in_dim(jnp.log(totals[0]), group * row_dev, row_dev, 0)

time: 157 us -> 134 us (0.85)
  waiting for transfers between devices: 83.9 us -> 0 us
  Pallas kernels: 17 us -> 99.8 us
  matrix products: 32.2 us -> 0 us
  local copies, waits for them, and re-layouts: 2.82 us -> 31.2 us
  between operations: 14.1 us -> 0.67 us
  other arithmetic: 4.31 us -> 1.36 us
  blocking collectives: 2.59 us -> 0 us
    all_gather x1 -> x0, waiting for transfers between devices: 83.9 us -> none  [plain_head(): pieces = lax.all_gather(normed[None], AXES, axis=0, tiled=True)]
    pallas_call x0 -> x1, Pallas kernels: none -> 73.8 us  [fused_head(): pl.pallas_call(functools.partial(head_kernel, sizes, cands), out_shape=(j...]
    dot_general x3 -> x0, matrix products: 32.2 us -> none  [the longest x1 26.4 us: plain_head(): jnp.einsum('vgrd,vdc->grc', pieces, weight, preferred_element_type=jnp.fl...]
    unnamed x3 -> x10, local copies, waits for them, and re-layouts: 0.68 us -> 27.6 us
    pallas_call x1, Pallas kernels: 17 us -> 26 us  [finish(): pl.pallas_call(functools.partial(finish_kernel, sizes), out_shape=(jax.Sh...]
    psum x1 -> x0, blocking collectives: 2.59 us -> none  [plain_head(): squared = lax.psum(jnp.sum(xf * xf, axis=1), 'vocab')]
    convert_element_type x1 -> x0, other arithmetic: 1.81 us -> none  [plain_head(): normed = (xf * scale[:, None] * gain_part[None, :]).astype(jnp.bfloat16)]
  transfers between devices with their start and end apart: 1 -> 0, of which waited for: 1 -> 0; matrix products, arithmetic and copies ran while one was open for 1% -> 0% of each run, Pallas kernels for 0% -> 0%
where the time goes in v2:
time: 134 us; the launch traced here: 133 us
  Pallas kernels  99.8 us (74%)
  local copies, waits for them, and re-layouts  31.2 us (23%)
  other arithmetic  1.36 us (1%)
    pallas_call x1, Pallas kernels, fused_head(): pl.pallas_call(functools.partial(head_kernel, sizes, cands), out_shape=(j...  73.8 us
    unnamed x10, local copies, waits for them, and re-layouts  27.6 us
    pallas_call x1, Pallas kernels, finish(): pl.pallas_call(functools.partial(finish_kernel, sizes), out_shape=(jax.Sh...  26 us

profile of v2, /device:TPU:0, one launch (start us, length us, event | category | flops | bytes accessed | tf_op | source)
XLA Modules:
  0.0 133.0 jit_solution(5896453982830428886)
XLA Ops:
  0.6 0.7 broadcast_subtract_fusion
  1.3 0.1 copy.10
  1.4 0.7 sub.18.wanted_ref
  2.1 0.0 copy-start.3
  2.1 0.0 copy-start.2
  2.1 24.7 %copy.11.head_hbm = bf16[4608,2000]{1,0:T(8,128)(2,1)} copy(bf16[4608,2000]{0,1:T(8,128)(2,1)} %param.7) | data formatting | bytes 36864000 | tf_op args[2]
  26.8 0.0 copy-done.3
  26.8 1.0 copy.12.prompt_ref
  27.8 0.0 copy-done.2
  27.8 0.6 reshape.28.gain_ref
  28.4 73.8 %shard_map.68 = (f32[4,1,256]{2,1,0:T(1,128)}, f32[1024,512]{1,0:T(8,128)}) custom-call(bf16[64,2304]{1,0:T(8,128)(2,1)} %hidden_ref.1, f32[2,1,2304]{2,1,0:T(1,128)} %reshape.28.gain_ref, bf16[4608,2000]{1,0:T(8,128)(2,1)} %copy.11.head_hbm, s32[1,512]{1,0:T(1,128)} %sub.18.wanted_ref, s32[1024,1]{1,0:T(8,128)} %copy.12.prompt_ref), custom_call_target="tpu_custom_call" | custom-call | tf_op jit(solution)/shard_map/pallas_call | solution.py:333
  102.2 0.0 copy-start
  102.3 1.6 %copy-done = f32[1024,512]{1,0:T(8,128)S(1)} copy-done((f32[1024,512]{1,0:T(8,128)S(1)}, f32[1024,512]{1,0:T(8,128)}, u32[]{:S(2)}) %copy-start) | copy-done | bytes 2097176
  103.8 0.0 copy-start.1
  103.8 0.7 copy-done.1
  104.5 26.0 %shard_map.69 = (f32[1,512]{1,0:T(1,128)S(1)}, f32[1,1024]{1,0:T(1,128)S(1)}) custom-call(f32[1,1024]{1,0:T(1,128)S(1)} %bitcast.4, f32[1024,512]{1,0:T(8,128)S(1)} %copy-done), custom_call_target="tpu_custom_call" | custom-call | tf_op jit(solution)/shard_map/pallas_call | solution.py:86
  130.5 0.6 fusion
  131.1 0.5 broadcast.12
  131.6 0.7 reduce.3
  132.3 0.1 reshape.30
  132.3 0.7 copy.13
Async XLA Ops:
  2.1 24.7 %copy-start.3 = (s32[1024]{0:T(1024)S(1)}, s32[1024]{0:T(1024)}, u32[]{:S(2)}) copy-start(s32[1024]{0:T(1024)} %param.9) | copy-start | bytes 12292
  2.1 25.7 %copy-start.2 = (f32[4608]{0:T(1024)S(1)}, f32[4608]{0:T(1024)}, u32[]{:S(2)}) copy-start(f32[4608]{0:T(1024)} %param.6) | copy-start | bytes 55300
  102.2 1.6 %copy-start = (f32[1024,512]{1,0:T(8,128)S(1)}, f32[1024,512]{1,0:T(8,128)}, u32[]{:S(2)}) copy-start(f32[1024,512]{1,0:T(8,128)} %get-tuple-element.7.terms_ref) | copy-start | bytes 6291460
  103.8 0.7 copy-start.1

commit v3 on v2

--- a/solution.py
+++ b/solution.py
@@ -68,8 +68,8 @@
     collect(sums_ref, sums_in, send_a, recv_a)
     total = jnp.sum(sums_in[...], axis=0)
     totals_ref[...] = total
-    part[...] = jnp.dot(
-        1.0 / total, terms_ref[...],
+    part[...] = lax.dot_general(
+        1.0 / total, terms_ref[...], (((1,), (1,)), ((), ())),
         precision=lax.Precision.HIGHEST, preferred_element_type=jnp.float32,
     )
     push(part, part_in, send_b, recv_b)
@@ -81,7 +81,7 @@
 def finish(sums, terms):
     sizes = tuple(lax.axis_size(axis) for axis in AXES)
     devices = sizes[0] * sizes[1] * sizes[2]
-    rows, picks = terms.shape
+    picks, rows = terms.shape
     vmem = pl.BlockSpec(memory_space=pltpu.VMEM)
     return pl.pallas_call(
         functools.partial(finish_kernel, sizes),
@@ -133,7 +133,7 @@
     picked = picked + jnp.dot(low, selector, preferred_element_type=jnp.float32)
     prompt_of = jnp.arange(wanted.shape[0], dtype=jnp.int32) // cands
     terms = jnp.where(row_prompt[:, None] == prompt_of[None, :], picked, 0.0)
-    return sums[None, :], terms
+    return sums[None, :], terms.T
 
 
 def head_kernel(
@@ -143,7 +143,7 @@
 ):
     depth = sizes[2]
     row_dev, cols = hidden_ref.shape
-    width, vocab_dev = head.shape
+    vocab_dev, width = head.shape
     span = depth * row_dev
     lanes = mine.shape[1]
     core = lax.axis_index("vocab")
@@ -222,9 +222,9 @@
         copy(core, sample, spot, line_send.at[step], (core, sample, at)).start()
     to_pair(sample, spot)
 
-    picks = wanted_ref.shape[1]
-    rows_of = lax.broadcasted_iota(jnp.int32, (vocab_dev, picks), 0)
-    selector[...] = jnp.where(rows_of == wanted_ref[...], 1.0, 0.0).astype(jnp.bfloat16)
+    picks = wanted_ref.shape[0]
+    columns_of = lax.broadcasted_iota(jnp.int32, (picks, vocab_dev), 1)
+    selector[...] = jnp.where(columns_of == wanted_ref[...], 1.0, 0.0).astype(jnp.bfloat16)
 
     for step in (1, depth - 1, *range(2, depth - 1)):
         at = (spot + step) % depth
@@ -279,20 +279,24 @@
                     to_second(first, at, 1)
                     to_pair(first, at)
 
-            raw = jnp.dot(
-                gathered[0, pl.ds(start, span), :], head[:cols, begin:end],
-                preferred_element_type=jnp.float32,
-            ) + jnp.dot(
-                gathered[1, pl.ds(start, span), :], head[cols:, begin:end],
-                preferred_element_type=jnp.float32,
+            raw = lax.dot_general(
+                gathered[0, pl.ds(start, span), :], head[begin:end, :cols],
+                (((1,), (1,)), ((), ())), preferred_element_type=jnp.float32,
+            ) + lax.dot_general(
+                gathered[1, pl.ds(start, span), :], head[begin:end, cols:],
+                (((1,), (1,)), ((), ())), preferred_element_type=jnp.float32,
             )
             exps = jnp.exp(CAP * jnp.tanh(raw / CAP))
             total = total + jnp.sum(exps, axis=1, keepdims=True)
             high = exps.astype(jnp.bfloat16)
             low = (exps - high.astype(jnp.float32)).astype(jnp.bfloat16)
-            part = jnp.dot(
-                high, selector[begin:end, :], preferred_element_type=jnp.float32
-            ) + jnp.dot(low, selector[begin:end, :], preferred_element_type=jnp.float32)
+            part = lax.dot_general(
+                selector[:, begin:end], high,
+                (((1,), (1,)), ((), ())), preferred_element_type=jnp.float32,
+            ) + lax.dot_general(
+                selector[:, begin:end], low,
+                (((1,), (1,)), ((), ())), preferred_element_type=jnp.float32,
+            )
             found = part if found is None else found + part
 
             for step in range(depth):
@@ -302,9 +306,9 @@
                     def _():
                         pass_on(across, (spot + order[step]) % depth)
 
-        prompt_of = lax.broadcasted_iota(jnp.int32, (span, picks), 1) // cands
-        terms_ref[pl.ds(start, span), :] = jnp.where(
-            prompt_ref[pl.ds(start, span), :] == prompt_of, found, 0.0
+        prompt_of = lax.broadcasted_iota(jnp.int32, (picks, span), 0) // cands
+        terms_ref[:, pl.ds(start, span)] = jnp.where(
+            prompt_ref[:, pl.ds(start, span)] == prompt_of, found, 0.0
         )
         sums_ref[column] = jnp.transpose(jnp.broadcast_to(total, (span, lanes)))[:1, :]
         return carry
@@ -334,14 +338,14 @@
         functools.partial(head_kernel, sizes, cands),
         out_shape=(
             jax.ShapeDtypeStruct((sizes[1], 1, span), jnp.float32),
-            jax.ShapeDtypeStruct((rows, picks), jnp.float32),
+            jax.ShapeDtypeStruct((picks, rows), jnp.float32),
         ),
         in_specs=[vmem, vmem, pl.BlockSpec(memory_space=pl.ANY), vmem, vmem],
         out_specs=(vmem, vmem),
         scratch_shapes=[
             pltpu.VMEM((sizes[0], rows, cols), jnp.bfloat16),
-            pltpu.VMEM(head.shape, jnp.bfloat16),
-            pltpu.VMEM((head.shape[1], picks), jnp.bfloat16),
+            pltpu.VMEM(head.shape[::-1], jnp.bfloat16),
+            pltpu.VMEM((picks, head.shape[1]), jnp.bfloat16),
             pltpu.VMEM((row_dev, lanes), jnp.float32),
             pltpu.VMEM((row_dev, lanes), jnp.float32),
             dma, dma, dma,
@@ -354,7 +358,7 @@
         compiler_params=pltpu.CompilerParams(
             collective_id=0, has_side_effects=True, vmem_limit_bytes=54 << 20
         ),
-    )(hidden, gain.reshape(sizes[0], 1, cols), head, wanted[None, :], row_prompt[:, None])
+    )(hidden, gain.reshape(sizes[0], 1, cols), head.T, wanted[:, None], row_prompt[None, :])
     return sums.reshape(1, rows), terms
 
 

time: 134 us -> 121 us (0.903)
  local copies, waits for them, and re-layouts: 31.2 us -> 6.44 us
  Pallas kernels: 99.8 us -> 112 us
    unnamed x10 -> x5, local copies, waits for them, and re-layouts: 27.6 us -> 2.93 us
    pallas_call x1, Pallas kernels: 73.8 us -> 85.6 us  [fused_head(): pl.pallas_call(functools.partial(head_kernel, sizes, cands), out_shape=(j...]
where the time goes in v3:
time: 121 us
  Pallas kernels  112 us (93%)
  local copies, waits for them, and re-layouts  6.44 us (5%)
  other arithmetic  1.36 us (1%)
    pallas_call x1, Pallas kernels, fused_head(): pl.pallas_call(functools.partial(head_kernel, sizes, cands), out_shape=(j...  85.6 us
    pallas_call x1, Pallas kernels, finish(): pl.pallas_call(functools.partial(finish_kernel, sizes), out_shape=(jax.Sh...  26.6 us
    unnamed x5, local copies, waits for them, and re-layouts  2.93 us

profile of v3, /device:TPU:0, one launch (start us, length us, event | category | flops | bytes accessed | tf_op | source)
XLA Modules:
  0.0 120.7 jit_solution(7976853142899762262)
XLA Ops:
  0.6 0.7 broadcast_subtract_fusion
  1.3 0.1 copy.9
  1.4 0.9 sub.19.wanted_ref
  2.3 1.3 %reshape.28.gain_ref = f32[2,1,2304]{2,1,0:T(1,128)} reshape(f32[4608]{0:T(1024)} %param.6) | data formatting | bytes 36864 | tf_op jit(solution)/shard_map/reshape | solution.py:361
  3.7 85.6 %shard_map.68 = (f32[4,1,256]{2,1,0:T(1,128)}, f32[512,1024]{1,0:T(8,128)}) custom-call(bf16[64,2304]{1,0:T(8,128)(2,1)} %hidden_ref.1, f32[2,1,2304]{2,1,0:T(1,128)} %reshape.28.gain_ref, bf16[2000,4608]{1,0:T(8,128)(2,1)} %bitcast.6, s32[512,1]{1,0:T(8,128)} %sub.19.wanted_ref, s32[1,1024]{1,0:T(1,128)} %bitcast.7), custom_call_target="tpu_custom_call" | custom-call | tf_op jit(solution)/shard_map/pallas_call | solution.py:337
  89.3 0.0 copy-start
  89.3 1.6 %copy-done = f32[512,1024]{1,0:T(8,128)S(1)} copy-done((f32[512,1024]{1,0:T(8,128)S(1)}, f32[512,1024]{1,0:T(8,128)}, u32[]{:S(2)}) %copy-start) | copy-done | bytes 2097176
  90.8 0.0 copy-start.1
  90.9 0.7 copy-done.1
  91.5 26.6 %shard_map.69 = (f32[1,512]{1,0:T(1,128)S(1)}, f32[1,1024]{1,0:T(1,128)S(1)}) custom-call(f32[1,1024]{1,0:T(1,128)S(1)} %bitcast.5, f32[512,1024]{1,0:T(8,128)S(1)} %copy-done), custom_call_target="tpu_custom_call" | custom-call | tf_op jit(solution)/shard_map/pallas_call | solution.py:86
  118.2 0.6 fusion
  118.8 0.5 broadcast.12
  119.3 0.7 reduce.3
  119.9 0.1 reshape.30
  120.0 0.7 copy.11
Async XLA Ops:
  89.3 1.6 %copy-start = (f32[512,1024]{1,0:T(8,128)S(1)}, f32[512,1024]{1,0:T(8,128)}, u32[]{:S(2)}) copy-start(f32[512,1024]{1,0:T(8,128)} %get-tuple-element.7.terms_ref) | copy-start | bytes 6291460
  90.8 0.7 copy-start.1

commit v4 on v3

--- a/solution.py
+++ b/solution.py
@@ -255,8 +255,6 @@
 
         @pl.when(t == 1)
         def _():
-            for step in order:
-                pass_on(second, (spot + step) % depth)
             for step in range(depth):
                 arrived(1 - core, first, (spot + step) % depth)
                 arrived(1 - core, second, (spot + step) % depth)
@@ -278,6 +276,7 @@
                     arrived(core, first, at)
                     to_second(first, at, 1)
                     to_pair(first, at)
+                    pass_on(second, at)
 
             raw = lax.dot_general(
                 gathered[0, pl.ds(start, span), :], head[begin:end, :cols],

time: 121 us -> 119 us (0.983)
  Pallas kernels: 112 us -> 110 us
    pallas_call x1, Pallas kernels: 85.6 us -> 81.9 us  [fused_head(): pl.pallas_call(functools.partial(head_kernel, sizes, cands), out_shape=(j...]
    pallas_call x1, Pallas kernels: 26.6 us -> 27.9 us  [finish(): pl.pallas_call(functools.partial(finish_kernel, sizes), out_shape=(jax.Sh...]
where the time goes in v4:
time: 119 us; the launch traced here: 118 us
  Pallas kernels  110 us (92%)
  local copies, waits for them, and re-layouts  6.44 us (5%)
  other arithmetic  1.36 us (1%)
    pallas_call x1, Pallas kernels, fused_head(): pl.pallas_call(functools.partial(head_kernel, sizes, cands), out_shape=(j...  81.9 us
    pallas_call x1, Pallas kernels, finish(): pl.pallas_call(functools.partial(finish_kernel, sizes), out_shape=(jax.Sh...  27.9 us
    unnamed x5, local copies, waits for them, and re-layouts  2.93 us

profile of v4, /device:TPU:0, one launch (start us, length us, event | category | flops | bytes accessed | tf_op | source)
XLA Modules:
  0.0 118.3 jit_solution(13338441452617243360)
XLA Ops:
  0.6 0.7 broadcast_subtract_fusion
  1.3 0.1 copy.9
  1.4 0.9 sub.19.wanted_ref
  2.3 1.3 %reshape.28.gain_ref = f32[2,1,2304]{2,1,0:T(1,128)} reshape(f32[4608]{0:T(1024)} %param.6) | data formatting | bytes 36864 | tf_op jit(solution)/shard_map/reshape | solution.py:360
  3.7 81.9 %shard_map.68 = (f32[4,1,256]{2,1,0:T(1,128)}, f32[512,1024]{1,0:T(8,128)}) custom-call(bf16[64,2304]{1,0:T(8,128)(2,1)} %hidden_ref.1, f32[2,1,2304]{2,1,0:T(1,128)} %reshape.28.gain_ref, bf16[2000,4608]{1,0:T(8,128)(2,1)} %bitcast.6, s32[512,1]{1,0:T(8,128)} %sub.19.wanted_ref, s32[1,1024]{1,0:T(1,128)} %bitcast.7), custom_call_target="tpu_custom_call" | custom-call | tf_op jit(solution)/shard_map/pallas_call | solution.py:336
  85.6 0.0 copy-start
  85.6 1.6 %copy-done = f32[512,1024]{1,0:T(8,128)S(1)} copy-done((f32[512,1024]{1,0:T(8,128)S(1)}, f32[512,1024]{1,0:T(8,128)}, u32[]{:S(2)}) %copy-start) | copy-done | bytes 2097176
  87.2 0.0 copy-start.1
  87.2 0.7 copy-done.1
  87.9 27.9 %shard_map.69 = (f32[1,512]{1,0:T(1,128)S(1)}, f32[1,1024]{1,0:T(1,128)S(1)}) custom-call(f32[1,1024]{1,0:T(1,128)S(1)} %bitcast.5, f32[512,1024]{1,0:T(8,128)S(1)} %copy-done), custom_call_target="tpu_custom_call" | custom-call | tf_op jit(solution)/shard_map/pallas_call | solution.py:86
  115.8 0.6 fusion
  116.4 0.5 broadcast.12
  116.9 0.7 reduce.3
  117.6 0.1 reshape.30
  117.7 0.7 copy.11
Async XLA Ops:
  85.6 1.6 %copy-start = (f32[512,1024]{1,0:T(8,128)S(1)}, f32[512,1024]{1,0:T(8,128)}, u32[]{:S(2)}) copy-start(f32[512,1024]{1,0:T(8,128)} %get-tuple-element.7.terms_ref) | copy-start | bytes 6291460
  87.2 0.7 copy-start.1
